TPU v7x, 32 devices: a whole 2x2x4 slice. The times are simulated.
32 devices in a mesh: grp: 4 (over y, x), dev: 8 (over z, core).
Axes of the slice: x: 2, y: 2, z: 4, core: 2. Of those that a mesh axis runs over, the one named last changes fastest.
Arguments:
- integral_slabs: bfloat16 [8, 512, 512], P('dev'), may hold values from -6 to 6
- slab_owner: int32 [8], replicated, may hold values from 0 to 7, each once
- pair_orbs: int32 [256, 2], P(('grp', 'dev')), may hold values from 0 to 7, all different within a row; in each aligned block of 8 rows (0 to 7, 8 to 15, ...) at most 2 rows name the same one
- domain_bases: bfloat16 [256, 512, 128], P(('grp', 'dev')), may hold values from -0.25 to 0.25
- amplitudes: bfloat16 [256, 128, 128], P(('grp', 'dev')), may hold values from -6 to 6
- coupled: int32 [256, 32], P(('grp', 'dev')), may hold values from 0 to 31
- coupled_len: int32 [256], P(('grp', 'dev')), may hold values from 1 to 32, as said below
Outputs:
- residual: float32 [256, 128, 128], P(('grp', 'dev'))
Inputs may be any that keep to these rules, and one draw needn't show every extreme that they name: `slab_owner`: a permutation of the positions. `pair_orbs`: the two orbitals of a pair differ; among the pairs of one device no orbital is named more than 2 times. `coupled_len`: pair 0 uses all 32 slots.
All inputs are finite; a program needn't handle non-finite values.
Results may differ from a plain program's by a relative error of at most 0.005.
Values may be sent and summed in bfloat16 or wider, within the bound.
No kernel may reach another device: no remote copies, remote signals or barrier semaphores. Data moves between devices by JAX's collectives and lax.ppermute only.
A program may use at most 128 MiB of HBM per device.

v0:
```python
import math

import jax
import jax.numpy as jnp
from jax import lax
from jax.sharding import PartitionSpec as P

NAUX = 512
NORB = 512
NPNO = 128


def side_positions(orbitals, slab_owner):
    flat = orbitals.reshape(-1)
    table = jnp.arange(slab_owner.shape[0], dtype=jnp.int32)
    return jnp.sum(jnp.where(flat[:, None] == table[None, :], slab_owner[None, :], 0), axis=1)


def half_pairs(halves):
    pair_count = halves.shape[0] // 2
    paired = halves.reshape(pair_count, 2, halves.shape[1], halves.shape[2])
    inverse_root = 1.0 / math.sqrt(NAUX)
    return (
        jnp.einsum("pan,pam->pnm", paired[:, 0], paired[:, 1], preferred_element_type=jnp.float32)
        * inverse_root
    )


def coupled_part(domain_bases, coupled, coupled_len, cand_bases, cand_amps):
    cand_count = cand_bases.shape[0]
    slot_live = (jnp.arange(coupled.shape[1])[None, :] < coupled_len[:, None]).astype(jnp.float32)
    matches = (
        coupled[:, :, None] == jnp.arange(cand_count, dtype=jnp.int32)[None, None, :]
    ).astype(jnp.float32)
    counts = jnp.einsum("ps,psc->pc", slot_live, matches)

    def one_pair(inputs):
        domain_basis, weights = inputs
        intersection = jnp.einsum(
            "ra,crb->cab", domain_basis, cand_bases, preferred_element_type=jnp.float32
        ).astype(jnp.bfloat16)
        projected = jnp.einsum(
            "cab,cbd->cad", intersection, cand_amps, preferred_element_type=jnp.float32
        ).astype(jnp.bfloat16)
        coupled_terms = jnp.einsum(
            "cad,ced->cae", projected, intersection, preferred_element_type=jnp.float32
        )
        return jnp.einsum("c,cae->ae", weights, coupled_terms)

    return lax.map(one_pair, (domain_bases, counts))


def on_device(
    integral_slabs, slab_owner, pair_orbs, domain_bases, amplitudes, coupled, coupled_len
):
    cand_bases, cand_amps = (
        lax.all_gather(domain_bases, "grp", axis=0, tiled=True),
        lax.all_gather(amplitudes, "grp", axis=0, tiled=True),
    )
    positions = side_positions(pair_orbs, slab_owner)
    n_dev = lax.axis_size("dev")
    side_count = positions.shape[0]
    capacity = max(2, (side_count + n_dev - 1) // n_dev)
    same_owner = positions[:, None] == positions[None, :]
    earlier = jnp.arange(side_count)[None, :] < jnp.arange(side_count)[:, None]
    slot_rank = jnp.sum(jnp.logical_and(same_owner, earlier), axis=1)
    side_bases = domain_bases[jnp.arange(side_count, dtype=jnp.int32) // 2]
    requests = jnp.zeros((n_dev, capacity) + domain_bases.shape[1:], jnp.bfloat16)
    requests = requests.at[positions, slot_rank].set(side_bases)
    own_slab = integral_slabs[0]
    products = jnp.einsum(
        "xn,dknp->dkxp",
        own_slab,
        lax.all_to_all(requests, "dev", split_axis=0, concat_axis=0, tiled=True),
        preferred_element_type=jnp.float32,
    ).astype(jnp.bfloat16)
    returned = lax.all_to_all(products, "dev", split_axis=0, concat_axis=0, tiled=True)
    halves = returned[positions, slot_rank]
    exchange = half_pairs(halves)
    coupled_sum = coupled_part(domain_bases, coupled, coupled_len, cand_bases, cand_amps)
    return exchange + NORB / NPNO * coupled_sum


def solution(mesh):
    in_specs = (
        P("dev", None, None),
        P(),
        P(("grp", "dev"), None),
        P(("grp", "dev"), None, None),
        P(("grp", "dev"), None, None),
        P(("grp", "dev"), None),
        P(("grp", "dev")),
    )
    out_specs = P(("grp", "dev"), None, None)
    return jax.shard_map(
        on_device, mesh=mesh, in_specs=in_specs, out_specs=out_specs, check_vma=False
    )
```

profile of v0, /device:TPU:0, one launch (start us, length us, event | category | flops | bytes accessed | tf_op | source)
XLA Modules:
  0.0 152.3 jit_solution(15315781980744005976)
XLA Ops:
  6.5 0.7 all-gather.5.cloned.1.call-update
  7.3 0.7 all-gather.3.cloned.1.call-update
  8.0 0.8 copy.22
  8.9 3.4 %gather_fusion = bf16[16,512,128]{2,1,0:T(8,128)(2,1)} fusion(bf16[8,512,128]{2,1,0:T(8,128)(2,1)} %param.12, s32[1024]{0:T(1024)S(1)} %pad_clamp_fusion), kind=kCustom, calls=%fused_computation | custom fusion | bytes 4194368 | tf_op jit(solution)/shard_map/gather | solution.py:67
  12.9 3.6 %scatter_fusion = bf16[8,2,512,128]{3,2,1,0:T(8,128)(2,1)S(1)} fusion(bf16[8,2,512,128]{3,2,1,0:T(8,128)(2,1)S(1)} %broadcast_in_dim.19, s32[16]{0:T(128)S(1)} %get-tuple-element.75, bf16[16,512,128]{2,1,0:T(8,128)(2,1)} %gather_fusion), kind=kCustom, calls=%fused_computation.2 | custom fusion | bytes 6291584 | tf_op jit(solution)/shard_map/scatter | solution.py:69
  16.5 2.6 %copy.23 = bf16[8,2,512,128]{2,3,1,0:T(8,128)(2,1)} copy(bf16[8,2,512,128]{3,2,1,0:T(8,128)(2,1)S(1)} %scatter_fusion) | data formatting | bytes 4194304 | tf_op jit(solution)/shard_map/scatter | solution.py:69
  19.1 6.5 %all-to-all-start = ((bf16[8,2,512,128]{2,3,1,0:T(8,128)(2,1)}), bf16[8,2,512,128]{2,3,1,0:T(8,128)(2,1)S(1)}, u32[]{:S(2)}, u32[]{:S(2)}) async-start(bf16[8,2,512,128]{2,3,1,0:T(8,128)(2,1)} %copy.23), calls=%async_computation | async-start | bytes 4194304 | tf_op jit(solution)/shard_map/all_to_all | solution.py:74
  25.9 48.8 %all-to-all-done = bf16[8,2,512,128]{2,3,1,0:T(8,128)(2,1)S(1)} async-done(((bf16[8,2,512,128]{2,3,1,0:T(8,128)(2,1)}), bf16[8,2,512,128]{2,3,1,0:T(8,128)(2,1)S(1)}, u32[]{:S(2)}, u32[]{:S(2)}) %all-to-all-start) | async-done | bytes 2097184 | tf_op jit(solution)/shard_map/all_to_all | solution.py:74
  74.7 2.6 %convert_bitcast_fusion = bf16[8,2,512,128]{2,3,1,0:T(8,128)(2,1)} fusion(bf16[8,2,512,128]{2,3,1,0:T(8,128)(2,1)S(1)} %all-to-all-done, bf16[1,512,512]{2,1,0:T(8,128)(2,1)S(1)} %copy-done), kind=kOutput, calls=%fused_computation.15 | convolution fusion | flops 1074790400 | bytes 4718592 | tf_op jit(solution)/shard_map/xn,dknp->dkxp/dot_general | solution.py:71
  77.3 4.3 %all-to-all-start.1 = ((bf16[8,2,512,128]{2,3,1,0:T(8,128)(2,1)}), bf16[8,2,512,128]{2,3,1,0:T(8,128)(2,1)}, u32[]{:S(2)}, u32[]{:S(2)}) async-start(bf16[8,2,512,128]{2,3,1,0:T(8,128)(2,1)} %convert_bitcast_fusion), calls=%async_computation.1 | async-start | bytes 4194304 | tf_op jit(solution)/shard_map/all_to_all | solution.py:77
  81.7 11.5 %all-gather.3.cloned.1.call-done = bf16[32,512,128]{2,1,0:T(8,128)(2,1)} async-done(((bf16[8,512,128]{2,1,0:T(8,128)(2,1)}), bf16[32,512,128]{2,1,0:T(8,128)(2,1)}) %all-gather.3.cloned.1.call-update) | async-done | bytes 4194320 | tf_op jit(solution)/shard_map/all_gather | solution.py:57
  93.1 48.8 %while.10 = (s32[]{:T(128)}, f32[8,128,128]{2,1,0:T(8,128)S(1)}, bf16[8,32]{1,0:T(8,128)(2,1)S(1)}, bf16[8,512,128]{2,1,0:T(8,128)(2,1)}, bf16[32,512,128]{2,1,0...) while((s32[]{:T(128)}, f32[8,128,128]{2,1,0:T(8,128)S(1)}, bf16[8,32]{1,0:T(8,128)(2,1)S(1)}, ...), condition=%wide.region_4.5_spmd, body=%wide.region_3.4_spmd.sunk | while | flops 807403520 | bytes 9765473 | solution.py:50
  93.1 3.0 %fusion.42 = bf16[32,128,128]{2,1,0:T(8,128)(2,1)S(1)} fusion(bf16[32,512,128]{2,1,0:T(8,128)(2,1)} %get-tuple-element.131, bf16[8,512,128]{2,1,0:T(8,128)(2,1)} %get-tuple-element.130, s32[]{:T(128)S(6)} %copy.45), kind=kOutput, calls=%fused_computation.7.clone.1 | convolution fusion | flops 537395200 | bytes 5373956 | tf_op jit(solution)/shard_map/while/body/eval_jaxpr/ra,crb->cab/dot_general | solution.py:39
  96.2 2.4 %fusion.43 = bf16[32,128,128]{2,1,0:T(8,128)(2,1)S(1)} fusion(bf16[32,128,128]{2,1,0:T(8,128)(2,1)S(1)} %fusion.42, bf16[32,128,128]{2,1,0:T(8,128)(2,1)} %get-tuple-element.132), kind=kOutput, calls=%fused_computation.8.clone.1 | convolution fusion | flops 268959744 | bytes 3145728 | tf_op jit(solution)/shard_map/while/body/eval_jaxpr/cad,ced->cae/dot_general | solution.py:45
  99.2 3.0 %fusion.42 = bf16[32,128,128]{2,1,0:T(8,128)(2,1)S(1)} fusion(bf16[32,512,128]{2,1,0:T(8,128)(2,1)} %get-tuple-element.131, bf16[8,512,128]{2,1,0:T(8,128)(2,1)} %get-tuple-element.130, s32[]{:T(128)S(6)} %copy.45), kind=kOutput, calls=%fused_computation.7.clone.1 | convolution fusion | flops 537395200 | bytes 5373956 | tf_op jit(solution)/shard_map/while/body/eval_jaxpr/ra,crb->cab/dot_general | solution.py:39
  102.3 2.4 %fusion.43 = bf16[32,128,128]{2,1,0:T(8,128)(2,1)S(1)} fusion(bf16[32,128,128]{2,1,0:T(8,128)(2,1)S(1)} %fusion.42, bf16[32,128,128]{2,1,0:T(8,128)(2,1)} %get-tuple-element.132), kind=kOutput, calls=%fused_computation.8.clone.1 | convolution fusion | flops 268959744 | bytes 3145728 | tf_op jit(solution)/shard_map/while/body/eval_jaxpr/cad,ced->cae/dot_general | solution.py:45
  105.3 3.0 %fusion.42 = bf16[32,128,128]{2,1,0:T(8,128)(2,1)S(1)} fusion(bf16[32,512,128]{2,1,0:T(8,128)(2,1)} %get-tuple-element.131, bf16[8,512,128]{2,1,0:T(8,128)(2,1)} %get-tuple-element.130, s32[]{:T(128)S(6)} %copy.45), kind=kOutput, calls=%fused_computation.7.clone.1 | convolution fusion | flops 537395200 | bytes 5373956 | tf_op jit(solution)/shard_map/while/body/eval_jaxpr/ra,crb->cab/dot_general | solution.py:39
  108.4 2.4 %fusion.43 = bf16[32,128,128]{2,1,0:T(8,128)(2,1)S(1)} fusion(bf16[32,128,128]{2,1,0:T(8,128)(2,1)S(1)} %fusion.42, bf16[32,128,128]{2,1,0:T(8,128)(2,1)} %get-tuple-element.132), kind=kOutput, calls=%fused_computation.8.clone.1 | convolution fusion | flops 268959744 | bytes 3145728 | tf_op jit(solution)/shard_map/while/body/eval_jaxpr/cad,ced->cae/dot_general | solution.py:45
  111.4 3.0 %fusion.42 = bf16[32,128,128]{2,1,0:T(8,128)(2,1)S(1)} fusion(bf16[32,512,128]{2,1,0:T(8,128)(2,1)} %get-tuple-element.131, bf16[8,512,128]{2,1,0:T(8,128)(2,1)} %get-tuple-element.130, s32[]{:T(128)S(6)} %copy.45), kind=kOutput, calls=%fused_computation.7.clone.1 | convolution fusion | flops 537395200 | bytes 5373956 | tf_op jit(solution)/shard_map/while/body/eval_jaxpr/ra,crb->cab/dot_general | solution.py:39
  114.5 2.4 %fusion.43 = bf16[32,128,128]{2,1,0:T(8,128)(2,1)S(1)} fusion(bf16[32,128,128]{2,1,0:T(8,128)(2,1)S(1)} %fusion.42, bf16[32,128,128]{2,1,0:T(8,128)(2,1)} %get-tuple-element.132), kind=kOutput, calls=%fused_computation.8.clone.1 | convolution fusion | flops 268959744 | bytes 3145728 | tf_op jit(solution)/shard_map/while/body/eval_jaxpr/cad,ced->cae/dot_general | solution.py:45
  116.8 0.7 fusion.44
  117.5 3.0 %fusion.42 = bf16[32,128,128]{2,1,0:T(8,128)(2,1)S(1)} fusion(bf16[32,512,128]{2,1,0:T(8,128)(2,1)} %get-tuple-element.131, bf16[8,512,128]{2,1,0:T(8,128)(2,1)} %get-tuple-element.130, s32[]{:T(128)S(6)} %copy.45), kind=kOutput, calls=%fused_computation.7.clone.1 | convolution fusion | flops 537395200 | bytes 5373956 | tf_op jit(solution)/shard_map/while/body/eval_jaxpr/ra,crb->cab/dot_general | solution.py:39
  120.6 2.4 %fusion.43 = bf16[32,128,128]{2,1,0:T(8,128)(2,1)S(1)} fusion(bf16[32,128,128]{2,1,0:T(8,128)(2,1)S(1)} %fusion.42, bf16[32,128,128]{2,1,0:T(8,128)(2,1)} %get-tuple-element.132), kind=kOutput, calls=%fused_computation.8.clone.1 | convolution fusion | flops 268959744 | bytes 3145728 | tf_op jit(solution)/shard_map/while/body/eval_jaxpr/cad,ced->cae/dot_general | solution.py:45
  122.9 0.7 fusion.44
  123.6 3.0 %fusion.42 = bf16[32,128,128]{2,1,0:T(8,128)(2,1)S(1)} fusion(bf16[32,512,128]{2,1,0:T(8,128)(2,1)} %get-tuple-element.131, bf16[8,512,128]{2,1,0:T(8,128)(2,1)} %get-tuple-element.130, s32[]{:T(128)S(6)} %copy.45), kind=kOutput, calls=%fused_computation.7.clone.1 | convolution fusion | flops 537395200 | bytes 5373956 | tf_op jit(solution)/shard_map/while/body/eval_jaxpr/ra,crb->cab/dot_general | solution.py:39
  126.7 2.4 %fusion.43 = bf16[32,128,128]{2,1,0:T(8,128)(2,1)S(1)} fusion(bf16[32,128,128]{2,1,0:T(8,128)(2,1)S(1)} %fusion.42, bf16[32,128,128]{2,1,0:T(8,128)(2,1)} %get-tuple-element.132), kind=kOutput, calls=%fused_computation.8.clone.1 | convolution fusion | flops 268959744 | bytes 3145728 | tf_op jit(solution)/shard_map/while/body/eval_jaxpr/cad,ced->cae/dot_general | solution.py:45
  129.7 3.0 %fusion.42 = bf16[32,128,128]{2,1,0:T(8,128)(2,1)S(1)} fusion(bf16[32,512,128]{2,1,0:T(8,128)(2,1)} %get-tuple-element.131, bf16[8,512,128]{2,1,0:T(8,128)(2,1)} %get-tuple-element.130, s32[]{:T(128)S(6)} %copy.45), kind=kOutput, calls=%fused_computation.7.clone.1 | convolution fusion | flops 537395200 | bytes 5373956 | tf_op jit(solution)/shard_map/while/body/eval_jaxpr/ra,crb->cab/dot_general | solution.py:39
  132.7 2.4 %fusion.43 = bf16[32,128,128]{2,1,0:T(8,128)(2,1)S(1)} fusion(bf16[32,128,128]{2,1,0:T(8,128)(2,1)S(1)} %fusion.42, bf16[32,128,128]{2,1,0:T(8,128)(2,1)} %get-tuple-element.132), kind=kOutput, calls=%fused_computation.8.clone.1 | convolution fusion | flops 268959744 | bytes 3145728 | tf_op jit(solution)/shard_map/while/body/eval_jaxpr/cad,ced->cae/dot_general | solution.py:45
  135.8 3.0 %fusion.42 = bf16[32,128,128]{2,1,0:T(8,128)(2,1)S(1)} fusion(bf16[32,512,128]{2,1,0:T(8,128)(2,1)} %get-tuple-element.131, bf16[8,512,128]{2,1,0:T(8,128)(2,1)} %get-tuple-element.130, s32[]{:T(128)S(6)} %copy.45), kind=kOutput, calls=%fused_computation.7.clone.1 | convolution fusion | flops 537395200 | bytes 5373956 | tf_op jit(solution)/shard_map/while/body/eval_jaxpr/ra,crb->cab/dot_general | solution.py:39
  138.8 2.4 %fusion.43 = bf16[32,128,128]{2,1,0:T(8,128)(2,1)S(1)} fusion(bf16[32,128,128]{2,1,0:T(8,128)(2,1)S(1)} %fusion.42, bf16[32,128,128]{2,1,0:T(8,128)(2,1)} %get-tuple-element.132), kind=kOutput, calls=%fused_computation.8.clone.1 | convolution fusion | flops 268959744 | bytes 3145728 | tf_op jit(solution)/shard_map/while/body/eval_jaxpr/cad,ced->cae/dot_general | solution.py:45
  141.9 2.3 %gather_fusion.1 = bf16[16,512,128]{1,2,0:T(8,128)(2,1)S(1)} fusion(bf16[8,2,512,128]{2,3,1,0:T(8,128)(2,1)} %all-to-all-done.1, s32[16]{0:T(128)S(1)} %get-tuple-element.74), kind=kCustom, calls=%fused_computation.1 | custom fusion | bytes 4194432 | tf_op jit(solution)/shard_map/gather | solution.py:78
  144.2 1.2 fusion.9
  (37 shorter events, 5.3 us)
Async XLA Ops:
  6.5 68.1 %copy-start = (bf16[1,512,512]{2,1,0:T(8,128)(2,1)S(1)}, bf16[1,512,512]{2,1,0:T(8,128)(2,1)}, u32[]{:S(2)}) copy-start(bf16[1,512,512]{2,1,0:T(8,128)(2,1)} %param.9) | copy-start | bytes 1572868
  6.5 75.1 %all-gather.5.cloned.1.call-start = ((), (), s32[]{:S(2)}) async-start(), calls=%async_computation.3 | async-start | bytes 1310720 | tf_op jit(solution)/shard_map/all_gather | solution.py:58
  7.3 85.9 %all-gather.3.cloned.1.call-start = ((), (), s32[]{:S(2)}) async-start(), calls=%async_computation.2 | async-start | bytes 5242880 | tf_op jit(solution)/shard_map/all_gather | solution.py:57
  8.9 3.4 %copy-start.2 = (s32[8]{0:T(128)S(1)}, s32[8]{0:T(128)}, u32[]{:S(2)}) copy-start(s32[8]{0:T(128)} %param.10) | copy-start | bytes 100
  19.1 6.5 %copy-start.3 = (s32[8]{0:T(128)S(1)}, s32[8]{0:T(128)}, u32[]{:S(2)}) copy-start(s32[8]{0:T(128)} %param.15) | copy-start | bytes 100
  19.1 6.5 %copy-start.1 = (s32[8,32]{1,0:T(8,128)S(1)}, s32[8,32]{1,0:T(8,128)}, u32[]{:S(2)}) copy-start(s32[8,32]{1,0:T(8,128)} %param.14) | copy-start | bytes 3076
  19.1 55.5 %all-to-all-start = ((bf16[8,2,512,128]{2,3,1,0:T(8,128)(2,1)}), bf16[8,2,512,128]{2,3,1,0:T(8,128)(2,1)S(1)}, u32[]{:S(2)}, u32[]{:S(2)}) async-start(bf16[8,2,512,128]{2,3,1,0:T(8,128)(2,1)} %copy.23), calls=%async_computation | async-start | bytes 4194304 | tf_op jit(solution)/shard_map/all_to_all | solution.py:74
  77.3 64.6 %all-to-all-start.1 = ((bf16[8,2,512,128]{2,3,1,0:T(8,128)(2,1)}), bf16[8,2,512,128]{2,3,1,0:T(8,128)(2,1)}, u32[]{:S(2)}, u32[]{:S(2)}) async-start(bf16[8,2,512,128]{2,3,1,0:T(8,128)(2,1)} %convert_bitcast_fusion), calls=%async_computation.1 | async-start | bytes 4194304 | tf_op jit(solution)/shard_map/all_to_all | solution.py:77
Sparse Core Ops, SparseCore 0:
  9.2 29.3 all-gather.4
  40.4 52.6 all-gather.2
where the time goes:
time: 153 us; the launch traced here: 152 us
  waiting for transfers between devices  61.7 us (40%)
  matrix products  52.6 us (34%)
  between operations  13.5 us (9%)
  local copies, waits for them, and re-layouts  13.1 us (9%)
  starting transfers between devices  10.8 us (7%)
    all_to_all x1, waiting for transfers between devices, on_device(): lax.all_to_all(requests, 'dev', split_axis=0, concat_axis=0, tiled=True)  48.8 us
    dot_general x8, matrix products, one_pair(): jnp.einsum('ra,crb->cab', domain_basis, cand_bases, preferred_element_typ...  24.1 us
    dot_general x8, matrix products, one_pair(): jnp.einsum('cad,ced->cae', projected, intersection, preferred_element_typ...  19 us
    all_gather x1, waiting for transfers between devices, on_device(): lax.all_gather(domain_bases, 'grp', axis=0, tiled=True)  11.5 us
    all_to_all x1, starting transfers between devices, on_device(): lax.all_to_all(requests, 'dev', split_axis=0, concat_axis=0, tiled=True)  6.46 us
    scatter x2, local copies, waits for them, and re-layouts, on_device(): requests = requests.at[positions, slot_rank].set(side_bases)  6.18 us
    dot_general x8, matrix products, one_pair(): return jnp.einsum('c,cae->ae', weights, coupled_terms)  5.39 us
    all_to_all x1, starting transfers between devices, on_device(): lax.all_to_all(products, 'dev', split_axis=0, concat_axis=0, tiled=True)  4.35 us
  transfers between devices with their start and end apart: 4, of which 2 were waited for; matrix products, arithmetic and copies ran while one was open for 41% of the time, Pallas kernels for 0%

commit v1 on v0

v1 whole, which is shorter than its diff:
```python
import functools
import math

import jax
import jax.numpy as jnp
from jax import lax
from jax.experimental import pallas as pl
from jax.experimental.pallas import tpu as pltpu
from jax.sharding import PartitionSpec as P

VMEM_LIMIT = 48 * 1024 * 1024
DECLARED = 20_000_000_000
SMEM_SPEC = pl.BlockSpec(memory_space=pltpu.SMEM)
VMEM_SPEC = pl.BlockSpec(memory_space=pltpu.VMEM)


def call_kernel(body, out_shape, scratch, name, smem_args, vmem_args, flops=DECLARED):
    return pl.pallas_call(
        body,
        out_shape=out_shape,
        in_specs=[SMEM_SPEC] * len(smem_args) + [VMEM_SPEC] * len(vmem_args),
        out_specs=VMEM_SPEC,
        scratch_shapes=scratch,
        compiler_params=pltpu.CompilerParams(vmem_limit_bytes=VMEM_LIMIT),
        cost_estimate=pl.CostEstimate(flops=flops, bytes_accessed=0, transcendentals=0),
        name=name,
    )(*smem_args, *vmem_args)


def coupled_kernel(first_ref, weight_ref, own_ref, *refs):
    *cand_refs, acc_ref, out_ref, inter_ref, proj_ref = refs
    pairs, pno, _ = out_ref.shape
    orbs = own_ref.shape[1]
    empty = jnp.zeros((pno, pno), jnp.bfloat16)
    size = cand_refs[0].shape[0]
    for j in range(0, size * len(cand_refs), 2):
        cand_ref, at = cand_refs[j // size], j % size
        first = first_ref[j // size] + at
        bases = jnp.concatenate([cand_ref[at, :orbs, :], cand_ref[at + 1, :orbs, :]], axis=1)
        inter = jnp.dot(own_ref[...], bases, preferred_element_type=jnp.float32).astype(jnp.bfloat16)
        inter_ref[:, j * pno : (j + 2) * pno] = inter
        amps = jnp.concatenate(
            [
                jnp.concatenate([cand_ref[at, orbs:, :], empty], axis=1),
                jnp.concatenate([empty, cand_ref[at + 1, orbs:, :]], axis=1),
            ],
            axis=0,
        )
        proj = jnp.dot(inter, amps, preferred_element_type=jnp.float32)
        for p in range(pairs):
            for c in range(2):
                block = proj[p * pno : (p + 1) * pno, c * pno : (c + 1) * pno]
                proj_ref[p * pno : (p + 1) * pno, (j + c) * pno : (j + c + 1) * pno] = (
                    block * weight_ref[p, first + c]
                ).astype(jnp.bfloat16)
    for p in range(pairs):
        rows = slice(p * pno, (p + 1) * pno)
        out_ref[p] = acc_ref[p] + lax.dot_general(
            proj_ref[rows, :], inter_ref[rows, :], (((1,), (1,)), ((), ())), preferred_element_type=jnp.float32
        )


def add_coupled(first, weights, own_t, chunks, acc, flops):
    rows, pno = own_t.shape[0], acc.shape[2]
    count = sum(chunk.shape[0] for chunk in chunks)
    return call_kernel(
        coupled_kernel,
        jax.ShapeDtypeStruct(acc.shape, jnp.float32),
        [pltpu.VMEM((rows, count * pno), jnp.bfloat16)] * 2,
        "coupled",
        (first, weights),
        (own_t, *chunks, acc),
        flops,
    )


def half_transforms(owner_ref, orbs_ref, turn_ref, slab_refs, base_ref, half_ref, uses_ref, base):
    pairs, _, pno = base_ref.shape
    sides = 2 * pairs

    def clear(k, carry):
        uses_ref[k, 0] = sides
        uses_ref[k, 1] = sides
        return carry

    def note(f, carry):
        k = turn_ref[owner_ref[orbs_ref[f // 2, f % 2]]]
        uses_ref[k, 1] = uses_ref[k, 0]
        uses_ref[k, 0] = f
        return carry

    lax.fori_loop(0, turn_ref.shape[0], clear, 0)
    lax.fori_loop(0, sides, note, 0)

    def both_sides(slab, k):
        one, two = uses_ref[k, 0], uses_ref[k, 1]
        last = pairs - 1
        bases = jnp.concatenate(
            [base_ref[jnp.minimum(one // 2, last)], base_ref[jnp.minimum(two // 2, last)]], axis=1
        )
        both = jnp.dot(slab, bases, preferred_element_type=jnp.float32).astype(jnp.bfloat16)
        half_ref[one] = both[:, :pno]
        half_ref[two] = both[:, pno:]

    for slab_ref in slab_refs:
        if slab_ref.shape[0] > 4:

            def step(k, carry, slab_ref=slab_ref, base=base):
                both_sides(slab_ref[k], base + k)
                return carry

            lax.fori_loop(0, slab_ref.shape[0], step, 0)
        else:
            for k in range(slab_ref.shape[0]):
                both_sides(slab_ref[k], base + k)
        base += slab_ref.shape[0]


def halves_kernel(owner_ref, orbs_ref, turn_ref, *refs):
    *slab_refs, base_ref, half_ref, uses_ref = refs
    half_transforms(owner_ref, orbs_ref, turn_ref, slab_refs, base_ref, half_ref, uses_ref, 0)


def exchange_kernel(scale, base, owner_ref, orbs_ref, turn_ref, *refs):
    *slab_refs, base_ref, early_ref, acc_ref, out_ref, half_ref, uses_ref = refs
    half_transforms(owner_ref, orbs_ref, turn_ref, slab_refs, base_ref, half_ref, uses_ref, base)
    for p in range(out_ref.shape[0]):
        left, right = [
            jnp.where(turn_ref[owner_ref[orbs_ref[p, side]]] < base, early_ref[2 * p + side], half_ref[2 * p + side])
            for side in range(2)
        ]
        product = lax.dot_general(left, right, (((0,), (0,)), ((), ())), preferred_element_type=jnp.float32)
        out_ref[p] = acc_ref[p] + product * scale


def first_halves(slab_owner, pair_orbs, turn, slabs, bases):
    pairs, _, pno = bases.shape
    return call_kernel(
        halves_kernel,
        jax.ShapeDtypeStruct((2 * pairs + 1, slabs[0].shape[1], pno), jnp.bfloat16),
        [pltpu.SMEM((turn.shape[0], 2), jnp.int32)],
        "halves",
        (slab_owner, pair_orbs, turn),
        (*slabs, bases),
        0,
    )


def add_exchange(slab_owner, pair_orbs, turn, base, slabs, bases, early, acc):
    return call_kernel(
        functools.partial(exchange_kernel, 1.0 / math.sqrt(slabs[0].shape[1]), base),
        jax.ShapeDtypeStruct(acc.shape, jnp.float32),
        [pltpu.VMEM(early.shape, jnp.bfloat16), pltpu.SMEM((turn.shape[0], 2), jnp.int32)],
        "exchange",
        (slab_owner, pair_orbs, turn),
        (*slabs, bases, early, acc),
        0,
    )


def after(value, *earlier):
    return lax.optimization_barrier((value,) + earlier)[0]


def slot_counts(coupled, coupled_len, cand_count, scale):
    live = jnp.arange(coupled.shape[1])[None, :] < coupled_len[:, None]
    hits = (coupled[:, :, None] == jnp.arange(cand_count, dtype=jnp.int32)[None, None, :]) & live[:, :, None]
    return jnp.sum(hits.astype(jnp.float32), axis=1) * scale


def on_device(integral_slabs, slab_owner, pair_orbs, domain_bases, amplitudes, coupled, coupled_len):
    n_grp, n_dev = lax.axis_size("grp"), lax.axis_size("dev")
    pairs, orbs, pno = domain_bases.shape
    group, me = lax.axis_index("grp"), lax.axis_index("dev")
    near1, near2, far = group ^ 1, group ^ 2, group ^ 3
    chips = n_dev // 2
    chip, core = me // 2, me % 2
    line = chips == 4

    half, part = pairs // 2, pairs // 4
    pack = lambda low, high: jnp.concatenate([domain_bases[low:high], amplitudes[low:high]], axis=1)
    own_lo, own_hi = pack(0, half), pack(half, pairs)

    def along_x(value):
        return lax.ppermute(value, "grp", [(g, g ^ 1) for g in range(n_grp)])

    def along_y(value):
        return lax.ppermute(value, "grp", [(g, g ^ 2) for g in range(n_grp)])

    def next_chip(value):
        return lax.ppermute(value, "dev", [(d, (d + 2) % n_dev) for d in range(n_dev)])

    def other_core(value):
        return lax.ppermute(value, "dev", [(d, d ^ 1) for d in range(n_dev)])

    weights = slot_counts(coupled, coupled_len, n_grp * pairs, orbs / pno)
    own_t = jnp.swapaxes(domain_bases, 1, 2).reshape(pairs * pno, orbs)

    def add(acc, *parts, flops=DECLARED):
        first = jnp.stack([source * pairs + low for source, low, _ in parts]).astype(jnp.int32)
        return add_coupled(first, weights, own_t, [chunk for _, _, chunk in parts], acc, flops)

    slab = integral_slabs[0]
    ring = chips <= 4

    x_lo, y_hi = along_x(own_lo), along_y(own_hi)
    x_hi1, y_lo1 = along_x(own_hi[:part]), along_y(own_lo[:part])
    far_hi, far_lo = along_x(y_hi), along_y(x_lo)

    acc = jnp.zeros((pairs, pno, pno), jnp.float32)
    acc = add(acc, (group, 0, own_lo), (group, half, own_hi))
    if ring:
        round1 = next_chip(slab)
        early = jnp.stack([slab, round1])
        early_swap = other_core(early)
        round2 = next_chip(after(round1, early_swap, x_lo, y_hi))
        acc = after(acc, early_swap)
    acc = add(acc, (near1, 0, x_lo), (near2, half, y_hi))
    acc = add(acc, (near1, half, x_hi1), (near2, 0, y_lo1), flops=0)
    if ring:
        round2 = after(round2, acc)
        swap2, round3 = other_core(round2), next_chip(round2)
        slabs = [early, early_swap, round2[None], swap2[None]]
        position = jnp.arange(n_dev, dtype=jnp.int32)
        steps = (chip - position // 2) % chips
        turn = jnp.where(steps < 2, steps, 2 * steps) + jnp.where(position % 2 == core, 0, jnp.where(steps < 2, 2, 1))
        ahead = 6
    else:
        gathered = lax.all_gather(slab, "dev", axis=0, tiled=False)
        ahead = n_dev // 2
        slabs, rest = [gathered[:ahead]], [gathered[ahead:]]
        swap2 = slab
        turn = jnp.arange(n_dev)
    turn = turn.astype(jnp.int32)
    x_hi2, y_lo2 = along_x(after(own_hi[part:], swap2)), along_y(after(own_lo[part:], swap2))
    halves = first_halves(slab_owner, pair_orbs, turn, slabs, after(domain_bases, acc))
    acc = after(acc, halves)
    acc = add(acc, (far, 0, far_lo), (far, half, far_hi), flops=0)
    if ring:
        round3 = after(round3, acc)
        rest = [round3[None], other_core(round3)[None]]
    acc = add_exchange(slab_owner, pair_orbs, turn, ahead, rest, domain_bases, halves, acc)
    return add(acc, (near1, half + part, x_hi2), (near2, part, y_lo2))


def solution(mesh):
    in_specs = (
        P("dev", None, None),
        P(),
        P(("grp", "dev"), None),
        P(("grp", "dev"), None, None),
        P(("grp", "dev"), None, None),
        P(("grp", "dev"), None),
        P(("grp", "dev")),
    )
    out_specs = P(("grp", "dev"), None, None)
    return jax.shard_map(
        on_device, mesh=mesh, in_specs=in_specs, out_specs=out_specs, check_vma=False
    )
```

time: 153 us -> 74.9 us (0.49)
  matrix products: 52.6 us -> 0 us
  waiting for transfers between devices: 61.7 us -> 23 us
  Pallas kernels: 0 us -> 27.5 us
  between operations: 13.5 us -> 0.2 us
  local copies, waits for them, and re-layouts: 13.1 us -> 7 us
  other arithmetic: 0.38 us -> 5.53 us
    dot_general x27 -> x0, matrix products: 52.6 us -> none  [the longest x8 24.1 us: one_pair(): jnp.einsum('ra,crb->cab', domain_basis, cand_bases, preferred_element_typ...]
    all_to_all x2 -> x0, waiting for transfers between devices: 48.8 us -> none  [the longest x1 48.8 us: on_device(): lax.all_to_all(requests, 'dev', split_axis=0, concat_axis=0, tiled=True)]
    pallas_call x0 -> x7, Pallas kernels: none -> 27.5 us  [call_kernel(): pl.pallas_call(body, out_shape=out_shape, in_specs=[SMEM_SPEC] * len(smem...]
    ppermute x0 -> x14, waiting for transfers between devices: none -> 23 us  [the longest x3 15.9 us: next_chip(): lax.ppermute(value, 'dev', [(d, (d + 2) % n_dev) for d in range(n_dev)])]
    all_gather x2 -> x0, waiting for transfers between devices: 11.5 us -> none  [the longest x1 11.5 us: on_device(): lax.all_gather(domain_bases, 'grp', axis=0, tiled=True)]
    ppermute x0 -> x14, starting transfers between devices: none -> 11.2 us  [the longest x4 4.05 us: along_x(): return lax.ppermute(value, 'grp', [(g, g ^ 1) for g in range(n_grp)])]
    all_to_all x2 -> x0, starting transfers between devices: 10.8 us -> none  [the longest x1 6.46 us: on_device(): lax.all_to_all(requests, 'dev', split_axis=0, concat_axis=0, tiled=True)]
    scatter x2 -> x0, local copies, waits for them, and re-layouts: 6.18 us -> none  [on_device(): requests = requests.at[positions, slot_rank].set(side_bases)]
  transfers between devices with their start and end apart: 4 -> 14, of which waited for: 2 -> 6; matrix products, arithmetic and copies ran while one was open for 41% -> 10% of each run, Pallas kernels for 0% -> 32%
where the time goes in v1:
time: 74.9 us; the launch traced here: 74.5 us
  Pallas kernels  27.5 us (37%)
  waiting for transfers between devices  23 us (31%)
  starting transfers between devices  11.2 us (15%)
  local copies, waits for them, and re-layouts  7 us (9%)
  other arithmetic  5.53 us (7%)
    pallas_call x7, Pallas kernels, call_kernel(): pl.pallas_call(body, out_shape=out_shape, in_specs=[SMEM_SPEC] * len(smem...  27.5 us
    ppermute x3, waiting for transfers between devices, next_chip(): lax.ppermute(value, 'dev', [(d, (d + 2) % n_dev) for d in range(n_dev)])  15.9 us
    unnamed x27, local copies, waits for them, and re-layouts  5.15 us
    ppermute x4, starting transfers between devices, along_x(): return lax.ppermute(value, 'grp', [(g, g ^ 1) for g in range(n_grp)])  4.05 us
    ppermute x4, starting transfers between devices, along_y(): return lax.ppermute(value, 'grp', [(g, g ^ 2) for g in range(n_grp)])  4.05 us
    ppermute x4, waiting for transfers between devices, along_y(): return lax.ppermute(value, 'grp', [(g, g ^ 2) for g in range(n_grp)])  4.03 us
    concatenate x4, other arithmetic, on_device(): jnp.concatenate([domain_bases[low:high], amplitudes[low:high]], axis=1)  3.62 us
    ppermute x3, waiting for transfers between devices, other_core(): return lax.ppermute(value, 'dev', [(d, d ^ 1) for d in range(n_dev)])  3.07 us
  transfers between devices with their start and end apart: 14, of which 6 were waited for; matrix products, arithmetic and copies ran while one was open for 10% of the time, Pallas kernels for 32%

profile of v1, /device:TPU:0, one launch (start us, length us, event | category | flops | bytes accessed | tf_op | source)
XLA Modules:
  0.0 74.5 jit_solution(922912663883929807)
XLA Ops:
  0.0 3.0 %collective-permute-start = (bf16[512,512]{1,0:T(8,128)(2,1)}, bf16[512,512]{1,0:T(8,128)(2,1)S(1)}, u32[]{:S(2)}, u32[]{:S(2)}) collective-permute-start(bf16[512,512]{1,0:T(8,128)(2,1)} %bitcast.25), channel_id=1, source_target_pairs={{0,2},{1,3},{2,4},{3,5},{4,6},{5,7},{6,0},{7,1},{8,10},{9,11},{10,... | collective-permute-start | bytes 1572872 | tf_op jit(solution)/shard_map/ppermute | solution.py:191
  3.0 1.3 %fusion.8 = (bf16[4,512,128]{2,1,0:T(8,128)(2,1)S(1)}, bf16[4,512,128]{2,1,0:T(8,128)(2,1)S(1)}) fusion(bf16[8,512,128]{2,1,0:T(8,128)(2,1)} %refs_2_.1), kind=kLoop, calls=%fused_computation.39 | loop fusion | bytes 2097152 | tf_op jit(solution)/shard_map/slice | solution.py:181
  4.3 0.9 %pad_maximum_fusion.2.refs_0_ = bf16[4,640,128]{2,1,0:T(8,128)(2,1)} fusion(bf16[4,128,128]{2,1,0:T(8,128)(2,1)S(1)} %get-tuple-element.27, bf16[4,512,128]{2,1,0:T(8,128)(2,1)S(1)} %get-tuple-element.21), kind=kLoop, calls=%fused_computation.6 | loop fusion | flops 1310720 | bytes 1310720 | tf_op jit(solution)/shard_map/concatenate | solution.py:181
  5.2 1.5 %collective-permute-start.2 = (bf16[4,640,128]{2,1,0:T(8,128)(2,1)}, bf16[4,640,128]{2,1,0:T(8,128)(2,1)}, u32[]{:S(2)}, u32[]{:S(2)}) collective-permute-start(bf16[4,640,128]{2,1,0:T(8,128)(2,1)} %pad_maximum_fusion.2.refs_0_), channel_id=1, source_target_pairs={{0,8},{8,0},{16,24},{24,16},{1,9},{9,1},{17,25},{25,17},{2,10},{10... | collective-permute-start | bytes 1966088 | tf_op jit(solution)/shard_map/ppermute | solution.py:185
  6.7 0.9 %pad_maximum_fusion.1.refs_1_ = bf16[4,640,128]{2,1,0:T(8,128)(2,1)} fusion(bf16[4,128,128]{2,1,0:T(8,128)(2,1)S(1)} %get-tuple-element.28, bf16[4,512,128]{2,1,0:T(8,128)(2,1)S(1)} %get-tuple-element.22), kind=kLoop, calls=%fused_computation.3 | loop fusion | flops 1310720 | bytes 1310720 | tf_op jit(solution)/shard_map/concatenate | solution.py:181
  7.6 1.5 %collective-permute-start.3 = (bf16[4,640,128]{2,1,0:T(8,128)(2,1)}, bf16[4,640,128]{2,1,0:T(8,128)(2,1)}, u32[]{:S(2)}, u32[]{:S(2)}) collective-permute-start(bf16[4,640,128]{2,1,0:T(8,128)(2,1)} %pad_maximum_fusion.1.refs_1_), channel_id=1, source_target_pairs={{0,16},{8,24},{16,0},{24,8},{1,17},{9,25},{17,1},{25,9},{2,18},{10... | collective-permute-start | bytes 1966088 | tf_op jit(solution)/shard_map/ppermute | solution.py:188
  9.2 0.9 %fusion.3 = (bf16[2,640,128]{2,1,0:T(8,128)(2,1)}, bf16[2,640,128]{2,1,0:T(8,128)(2,1)}) fusion(bf16[4,512,128]{2,1,0:T(8,128)(2,1)S(1)} %get-tuple-element.22, bf16[4,128,128]{2,1,0:T(8,128)(2,1)S(1)} %get-tuple-element.28), kind=kLoop, calls=%fused_computation.14 | loop fusion | flops 1310720 | bytes 1310720 | tf_op jit(solution)/shard_map/concatenate | solution.py:181
  10.1 0.5 collective-permute-start.5
  10.6 0.9 %fusion.1 = (bf16[2,640,128]{2,1,0:T(8,128)(2,1)}, bf16[2,640,128]{2,1,0:T(8,128)(2,1)}) fusion(bf16[4,512,128]{2,1,0:T(8,128)(2,1)S(1)} %get-tuple-element.21, bf16[4,128,128]{2,1,0:T(8,128)(2,1)S(1)} %get-tuple-element.27), kind=kLoop, calls=%fused_computation.12 | loop fusion | flops 1310720 | bytes 1310720 | tf_op jit(solution)/shard_map/concatenate | solution.py:181
  12.0 0.5 copy.11
  12.9 4.3 %collective-permute-done = bf16[512,512]{1,0:T(8,128)(2,1)S(1)} collective-permute-done((bf16[512,512]{1,0:T(8,128)(2,1)}, bf16[512,512]{1,0:T(8,128)(2,1)S(1)}, u32[]{:S(2)}, u32[]{:S(2)}) %collective-permute-start) | collective-permute-done | bytes 524320 | tf_op jit(solution)/shard_map/ppermute | solution.py:191
  17.2 0.8 %copy-done.7 = bf16[512,512]{1,0:T(8,128)(2,1)} copy-done((bf16[512,512]{1,0:T(8,128)(2,1)}, bf16[512,512]{1,0:T(8,128)(2,1)S(1)}, u32[]{:S(2)}) %copy-start.7) | copy-done | bytes 524312
  18.0 1.3 %pad_maximum_fusion.refs_0_ = bf16[2,512,512]{2,1,0:T(8,128)(2,1)S(1)} fusion(bf16[1,512,512]{2,1,0:T(8,128)(2,1)} %bitcast.26, bf16[1,512,512]{2,1,0:T(8,128)(2,1)} %param.7), kind=kLoop, calls=%fused_computation | loop fusion | flops 524288 | bytes 2097152 | tf_op jit(solution)/shard_map/stack | solution.py:214
  19.4 4.7 %coupled.5.refs_2_ = f32[8,128,128]{2,1,0:T(8,128)S(1)} custom-call(s32[2]{0:T(128)S(1)} %pad_add_fusion.3.first_ref, f32[8,32]{1,0:T(8,128)S(1)} %broadcast_multiply_fusion.weight_ref, bf16[1024,512]{1,0:T(8,128)(2,1)S(1)} %bitcast.19, bf16[4,640,128]{2,1,0:T(8,128)(2,1)} %pad_maximum_fusion.2.refs_0_, bf16[4,640,128]{2,1,0:T(8,128)(2,1)} %pad_maximum_fusion.1.refs_1_, ...), custom_call_target="tpu_custom_call" | custom-call | flops 20000000000 | tf_op jit(solution)/shard_map/coupled/pallas_call | solution.py:18
  24.1 0.8 %copy-done.5 = f32[8,128,128]{2,1,0:T(8,128)} copy-done((f32[8,128,128]{2,1,0:T(8,128)}, f32[8,128,128]{2,1,0:T(8,128)S(1)}, u32[]{:S(2)}) %copy-start.5) | copy-done | bytes 524312
  25.0 1.5 %collective-permute-start.11 = (bf16[4,640,128]{2,1,0:T(8,128)(2,1)}, bf16[4,640,128]{2,1,0:T(8,128)(2,1)}, u32[]{:S(2)}, u32[]{:S(2)}) collective-permute-start(bf16[4,640,128]{2,1,0:T(8,128)(2,1)} %collective-permute-done.2.refs_0_), channel_id=1, source_target_pairs={{0,16},{8,24},{16,0},{24,8},{1,17},{9,25},{17,1},{25,9},{2,18},{10... | collective-permute-start | bytes 1966088 | tf_op jit(solution)/shard_map/ppermute | solution.py:188
  26.6 1.5 %collective-permute-start.12 = (bf16[4,640,128]{2,1,0:T(8,128)(2,1)}, bf16[4,640,128]{2,1,0:T(8,128)(2,1)}, u32[]{:S(2)}, u32[]{:S(2)}) collective-permute-start(bf16[4,640,128]{2,1,0:T(8,128)(2,1)} %collective-permute-done.3.refs_1_), channel_id=1, source_target_pairs={{0,8},{8,0},{16,24},{24,16},{1,9},{9,1},{17,25},{25,17},{2,10},{10... | collective-permute-start | bytes 1966088 | tf_op jit(solution)/shard_map/ppermute | solution.py:185
  28.1 1.0 %copy-done.6 = f32[8,128,128]{2,1,0:T(8,128)S(1)} copy-done((f32[8,128,128]{2,1,0:T(8,128)S(1)}, f32[8,128,128]{2,1,0:T(8,128)}, u32[]{:S(2)}) %copy-start.6) | copy-done | bytes 524312
  29.1 4.7 %coupled.6.refs_2_ = f32[8,128,128]{2,1,0:T(8,128)S(1)} custom-call(s32[2]{0:T(128)S(1)} %pad_add_fusion.2.first_ref, f32[8,32]{1,0:T(8,128)S(1)} %broadcast_multiply_fusion.weight_ref, bf16[1024,512]{1,0:T(8,128)(2,1)S(1)} %bitcast.20, bf16[4,640,128]{2,1,0:T(8,128)(2,1)} %collective-permute-done.2.refs_0_, ...), custom_call_target="tpu_custom_call" | custom-call | flops 20000000000 | tf_op jit(solution)/shard_map/coupled/pallas_call | solution.py:18
  33.8 2.7 %coupled.7.refs_2_ = f32[8,128,128]{2,1,0:T(8,128)S(1)} custom-call(s32[2]{0:T(128)S(1)} %pad_add_fusion.1.first_ref, f32[8,32]{1,0:T(8,128)S(1)} %broadcast_multiply_fusion.weight_ref, bf16[1024,512]{1,0:T(8,128)(2,1)S(1)} %bitcast.21, bf16[2,640,128]{2,1,0:T(8,128)(2,1)S(1)} %collective-permute-done.5.refs_0_, ...), custom_call_target="tpu_custom_call" | custom-call | tf_op jit(solution)/shard_map/coupled/pallas_call | solution.py:18
  36.6 0.8 %copy-done.2 = f32[8,128,128]{2,1,0:T(8,128)} copy-done((f32[8,128,128]{2,1,0:T(8,128)}, f32[8,128,128]{2,1,0:T(8,128)S(1)}, u32[]{:S(2)}) %copy-start.2) | copy-done | bytes 524312
  37.3 6.6 %collective-permute-done.4 = bf16[512,512]{1,0:T(8,128)(2,1)} collective-permute-done((bf16[512,512]{1,0:T(8,128)(2,1)}, bf16[512,512]{1,0:T(8,128)(2,1)}, u32[]{:S(2)}, u32[]{:S(2)}) %collective-permute-start.4) | collective-permute-done | bytes 524320 | tf_op jit(solution)/shard_map/ppermute | solution.py:191
  44.1 2.1 %collective-permute-done.7 = bf16[512,512]{1,0:T(8,128)(2,1)} collective-permute-done((bf16[512,512]{1,0:T(8,128)(2,1)}, bf16[512,512]{1,0:T(8,128)(2,1)}, u32[]{:S(2)}, u32[]{:S(2)}) %collective-permute-start.7) | collective-permute-done | bytes 524320 | tf_op jit(solution)/shard_map/ppermute | solution.py:194
  46.2 4.5 %halves.1.refs_3_ = bf16[17,512,128]{2,1,0:T(8,128)(2,1)} custom-call(s32[8]{0:T(128)S(1)} %copy-done.4, s32[8,2]{1,0:T(8,128)S(1)} %copy.13.orbs_ref, s32[8]{0:T(128)S(1)} %fusion.5.turn_ref, bf16[2,512,512]{2,1,0:T(8,128)(2,1)S(1)} %pad_maximum_fusion.refs_0_, bf16[2,512,512]{2,1,0:T(8,128)(2,1)} %collective-permute-done.1.refs_1_, ...), custom_call_target="tpu_custom_call" | custom-call | tf_op jit(solution)/shard_map/halves/pallas_call | solution.py:18
  50.7 4.7 %coupled.8.refs_4_ = f32[8,128,128]{2,1,0:T(8,128)S(1)} custom-call(s32[2]{0:T(128)S(1)} %pad_add_fusion.4.first_ref, f32[8,32]{1,0:T(8,128)S(1)} %broadcast_multiply_fusion.weight_ref, bf16[1024,512]{1,0:T(8,128)(2,1)S(1)} %bitcast.22, bf16[4,640,128]{2,1,0:T(8,128)(2,1)} %collective-permute-done.11.refs_0_, ...), custom_call_target="tpu_custom_call" | custom-call | tf_op jit(solution)/shard_map/coupled/pallas_call | solution.py:18
  55.4 5.0 %collective-permute-done.10 = bf16[512,512]{1,0:T(8,128)(2,1)} collective-permute-done((bf16[512,512]{1,0:T(8,128)(2,1)}, bf16[512,512]{1,0:T(8,128)(2,1)}, u32[]{:S(2)}, u32[]{:S(2)}) %collective-permute-start.10) | collective-permute-done | bytes 524320 | tf_op jit(solution)/shard_map/ppermute | solution.py:191
  60.9 0.5 collective-permute-start.8
  61.5 1.0 %collective-permute-done.13 = bf16[512,512]{1,0:T(8,128)(2,1)S(1)} collective-permute-done((bf16[512,512]{1,0:T(8,128)(2,1)}, bf16[512,512]{1,0:T(8,128)(2,1)S(1)}, u32[]{:S(2)}, u32[]{:S(2)}) %collective-permute-start.13) | collective-permute-done | bytes 524320 | tf_op jit(solution)/shard_map/ppermute | solution.py:194
  62.5 1.6 %copy-done.1 = bf16[17,512,128]{2,1,0:T(8,128)(2,1)S(1)} copy-done((bf16[17,512,128]{2,1,0:T(8,128)(2,1)S(1)}, bf16[17,512,128]{2,1,0:T(8,128)(2,1)}, u32[]{:S(2)}) %copy-start.1) | copy-done | bytes 2228248
  64.1 2.7 %exchange.1.refs_2_ = f32[8,128,128]{2,1,0:T(8,128)S(1)} custom-call(s32[8]{0:T(128)S(1)} %copy-done.4, s32[8,2]{1,0:T(8,128)S(1)} %copy.13.orbs_ref, s32[8]{0:T(128)S(1)} %fusion.5.turn_ref, bf16[1,512,512]{2,1,0:T(8,128)(2,1)} %bitcast.16.refs_0_, bf16[1,512,512]{2,1,0:T(8,128)(2,1)S(1)} %bitcast.24, bf16[8,512,128]{2,1,0:T(8,128)(2,1)S(1)} %copy-done, ...), custom_call_target="tpu_custom_call" | custom-call | tf_op jit(solution)/shard_map/exchange/pallas_call | solution.py:18
  66.8 4.0 %collective-permute-done.9.refs_1_ = bf16[2,640,128]{2,1,0:T(8,128)(2,1)} collective-permute-done((bf16[2,640,128]{2,1,0:T(8,128)(2,1)}, bf16[2,640,128]{2,1,0:T(8,128)(2,1)}, u32[]{:S(2)}, u32[]{:S(2)}) %collective-permute-start.9) | collective-permute-done | bytes 327712 | tf_op jit(solution)/shard_map/ppermute | solution.py:188
  70.8 3.6 %coupled.9 = f32[8,128,128]{2,1,0:T(8,128)} custom-call(s32[2]{0:T(128)S(1)} %pad_add_fusion.first_ref, f32[8,32]{1,0:T(8,128)S(1)} %broadcast_multiply_fusion.weight_ref, bf16[1024,512]{1,0:T(8,128)(2,1)S(1)} %bitcast.23, bf16[2,640,128]{2,1,0:T(8,128)(2,1)} %collective-permute-done.8.refs_0_, bf16[2,640,128]{2,1,0:T(8,128)(2,1)} %collective-permute-done.9.refs_1_, ...), custom_call_target="tpu_custom_call" | custom-call | flops 20000000000 | tf_op jit(solution)/shard_map/coupled/pallas_call | solution.py:18
  (48 shorter events, 1.9 us)
Async XLA Ops:
  0.0 4.3 %copy-start.9 = (bf16[8,128,128]{2,1,0:T(8,128)(2,1)S(1)}, bf16[8,128,128]{2,1,0:T(8,128)(2,1)}, u32[]{:S(2)}) copy-start(bf16[8,128,128]{2,1,0:T(8,128)(2,1)} %param.11) | copy-start | bytes 786436
  0.0 17.2 %collective-permute-start = (bf16[512,512]{1,0:T(8,128)(2,1)}, bf16[512,512]{1,0:T(8,128)(2,1)S(1)}, u32[]{:S(2)}, u32[]{:S(2)}) collective-permute-start(bf16[512,512]{1,0:T(8,128)(2,1)} %bitcast.25), channel_id=1, source_target_pairs={{0,2},{1,3},{2,4},{3,5},{4,6},{5,7},{6,0},{7,1},{8,10},{9,11},{10,... | collective-permute-start | bytes 1572872 | tf_op jit(solution)/shard_map/ppermute | solution.py:191
  5.2 19.8 %collective-permute-start.2 = (bf16[4,640,128]{2,1,0:T(8,128)(2,1)}, bf16[4,640,128]{2,1,0:T(8,128)(2,1)}, u32[]{:S(2)}, u32[]{:S(2)}) collective-permute-start(bf16[4,640,128]{2,1,0:T(8,128)(2,1)} %pad_maximum_fusion.2.refs_0_), channel_id=1, source_target_pairs={{0,8},{8,0},{16,24},{24,16},{1,9},{9,1},{17,25},{25,17},{2,10},{10... | collective-permute-start | bytes 1966088 | tf_op jit(solution)/shard_map/ppermute | solution.py:185
  7.6 4.4 %copy-start = (bf16[8,512,128]{2,1,0:T(8,128)(2,1)S(1)}, bf16[8,512,128]{2,1,0:T(8,128)(2,1)}, u32[]{:S(2)}) copy-start(bf16[8,512,128]{2,1,0:T(8,128)(2,1)} %refs_2_.1) | copy-start | bytes 3145732
  7.6 18.9 %collective-permute-start.3 = (bf16[4,640,128]{2,1,0:T(8,128)(2,1)}, bf16[4,640,128]{2,1,0:T(8,128)(2,1)}, u32[]{:S(2)}, u32[]{:S(2)}) collective-permute-start(bf16[4,640,128]{2,1,0:T(8,128)(2,1)} %pad_maximum_fusion.1.refs_1_), channel_id=1, source_target_pairs={{0,16},{8,24},{16,0},{24,8},{1,17},{9,25},{17,1},{25,9},{2,18},{10... | collective-permute-start | bytes 1966088 | tf_op jit(solution)/shard_map/ppermute | solution.py:188
  10.1 23.7 %collective-permute-start.5 = (bf16[2,640,128]{2,1,0:T(8,128)(2,1)}, bf16[2,640,128]{2,1,0:T(8,128)(2,1)S(1)}, u32[]{:S(2)}, u32[]{:S(2)}) collective-permute-start(bf16[2,640,128]{2,1,0:T(8,128)(2,1)} %get-tuple-element.25), channel_id=1, source_target_pairs={{0,8},{8,0},{16,24},{24,16},{1,9},{9,1},{17,25},{25,17},{2,10},{10... | collective-permute-start | bytes 983048 | tf_op jit(solution)/shard_map/ppermute | solution.py:185
  11.5 1.1 %copy-start.12 = (s32[8]{0:T(128)S(1)}, s32[8]{0:T(128)}, u32[]{:S(2)}) copy-start(s32[8]{0:T(128)} %param.13) | copy-start | bytes 100
  11.5 1.2 %copy-start.10 = (s32[8,32]{1,0:T(8,128)S(1)}, s32[8,32]{1,0:T(8,128)}, u32[]{:S(2)}) copy-start(s32[8,32]{1,0:T(8,128)} %param.12) | copy-start | bytes 3076
  11.5 22.3 %collective-permute-start.6 = (bf16[2,640,128]{2,1,0:T(8,128)(2,1)}, bf16[2,640,128]{2,1,0:T(8,128)(2,1)}, u32[]{:S(2)}, u32[]{:S(2)}) collective-permute-start(bf16[2,640,128]{2,1,0:T(8,128)(2,1)} %get-tuple-element.24), channel_id=1, source_target_pairs={{0,16},{8,24},{16,0},{24,8},{1,17},{9,25},{17,1},{25,9},{2,18},{10... | collective-permute-start | bytes 983048 | tf_op jit(solution)/shard_map/ppermute | solution.py:188
  17.2 0.8 %copy-start.7 = (bf16[512,512]{1,0:T(8,128)(2,1)}, bf16[512,512]{1,0:T(8,128)(2,1)S(1)}, u32[]{:S(2)}) copy-start(bf16[512,512]{1,0:T(8,128)(2,1)S(1)} %collective-permute-done) | copy-start | bytes 1572868
  19.3 8.8 %collective-permute-start.1 = (bf16[2,512,512]{2,1,0:T(8,128)(2,1)S(1)}, bf16[2,512,512]{2,1,0:T(8,128)(2,1)}, u32[]{:S(2)}, u32[]{:S(2)}) collective-permute-start(bf16[2,512,512]{2,1,0:T(8,128)(2,1)S(1)} %pad_maximum_fusion.refs_0_), channel_id=1, source_target_pairs={{0,1},{1,0},{2,3},{3,2},{4,5},{5,4},{6,7},{7,6},{8,9},{9,8},{10,11... | collective-permute-start | bytes 3145736 | tf_op jit(solution)/shard_map/ppermute | solution.py:194
  24.1 0.8 %copy-start.5 = (f32[8,128,128]{2,1,0:T(8,128)}, f32[8,128,128]{2,1,0:T(8,128)S(1)}, u32[]{:S(2)}) copy-start(f32[8,128,128]{2,1,0:T(8,128)S(1)} %coupled.5.refs_2_) | copy-start | bytes 1572868
  25.0 25.7 %collective-permute-start.11 = (bf16[4,640,128]{2,1,0:T(8,128)(2,1)}, bf16[4,640,128]{2,1,0:T(8,128)(2,1)}, u32[]{:S(2)}, u32[]{:S(2)}) collective-permute-start(bf16[4,640,128]{2,1,0:T(8,128)(2,1)} %collective-permute-done.2.refs_0_), channel_id=1, source_target_pairs={{0,16},{8,24},{16,0},{24,8},{1,17},{9,25},{17,1},{25,9},{2,18},{10... | collective-permute-start | bytes 1966088 | tf_op jit(solution)/shard_map/ppermute | solution.py:188
  26.6 24.1 %collective-permute-start.12 = (bf16[4,640,128]{2,1,0:T(8,128)(2,1)}, bf16[4,640,128]{2,1,0:T(8,128)(2,1)}, u32[]{:S(2)}, u32[]{:S(2)}) collective-permute-start(bf16[4,640,128]{2,1,0:T(8,128)(2,1)} %collective-permute-done.3.refs_1_), channel_id=1, source_target_pairs={{0,8},{8,0},{16,24},{24,16},{1,9},{9,1},{17,25},{25,17},{2,10},{10... | collective-permute-start | bytes 1966088 | tf_op jit(solution)/shard_map/ppermute | solution.py:185
  28.1 15.9 %collective-permute-start.4 = (bf16[512,512]{1,0:T(8,128)(2,1)}, bf16[512,512]{1,0:T(8,128)(2,1)}, u32[]{:S(2)}, u32[]{:S(2)}) collective-permute-start(bf16[512,512]{1,0:T(8,128)(2,1)} %copy-done.7), channel_id=1, source_target_pairs={{0,2},{1,3},{2,4},{3,5},{4,6},{5,7},{6,0},{7,1},{8,10},{9,11},{10,... | collective-permute-start | bytes 1572872 | tf_op jit(solution)/shard_map/ppermute | solution.py:191
  28.1 1.0 %copy-start.6 = (f32[8,128,128]{2,1,0:T(8,128)S(1)}, f32[8,128,128]{2,1,0:T(8,128)}, u32[]{:S(2)}) copy-start(f32[8,128,128]{2,1,0:T(8,128)} %copy-done.5) | copy-start | bytes 1572868
  33.8 10.2 %copy-start.11 = (s32[8,2]{0,1:T(2,128)S(1)}, s32[8,2]{0,1:T(2,128)}, u32[]{:S(2)}) copy-start(s32[8,2]{0,1:T(2,128)} %param.9) | copy-start | bytes 196
  33.8 12.4 %copy-start.4 = (s32[8]{0:T(128)S(1)}, s32[8]{0:T(128)}, u32[]{:S(2)}) copy-start(s32[8]{0:T(128)} %owner_ref.3) | copy-start | bytes 100
  36.5 0.8 %copy-start.2 = (f32[8,128,128]{2,1,0:T(8,128)}, f32[8,128,128]{2,1,0:T(8,128)S(1)}, u32[]{:S(2)}) copy-start(f32[8,128,128]{2,1,0:T(8,128)S(1)} %coupled.7.refs_2_) | copy-start | bytes 1572868
  43.9 2.3 %collective-permute-start.7 = (bf16[512,512]{1,0:T(8,128)(2,1)}, bf16[512,512]{1,0:T(8,128)(2,1)}, u32[]{:S(2)}, u32[]{:S(2)}) collective-permute-start(bf16[512,512]{1,0:T(8,128)(2,1)} %collective-permute-done.4), channel_id=1, source_target_pairs={{0,1},{1,0},{2,3},{3,2},{4,5},{5,4},{6,7},{7,6},{8,9},{9,8},{10,11... | collective-permute-start | bytes 1572872 | tf_op jit(solution)/shard_map/ppermute | solution.py:194
  43.9 16.5 %collective-permute-start.10 = (bf16[512,512]{1,0:T(8,128)(2,1)}, bf16[512,512]{1,0:T(8,128)(2,1)}, u32[]{:S(2)}, u32[]{:S(2)}) collective-permute-start(bf16[512,512]{1,0:T(8,128)(2,1)} %collective-permute-done.4), channel_id=1, source_target_pairs={{0,2},{1,3},{2,4},{3,5},{4,6},{5,7},{6,0},{7,1},{8,10},{9,11},{10,... | collective-permute-start | bytes 1572872 | tf_op jit(solution)/shard_map/ppermute | solution.py:191
  46.2 4.5 %copy-start.3 = (f32[8,128,128]{2,1,0:T(8,128)S(1)}, f32[8,128,128]{2,1,0:T(8,128)}, u32[]{:S(2)}) copy-start(f32[8,128,128]{2,1,0:T(8,128)} %copy-done.2) | copy-start | bytes 1572868
  50.7 10.2 %copy-start.8 = (bf16[2,640,128]{2,1,0:T(8,128)(2,1)S(1)}, bf16[2,640,128]{2,1,0:T(8,128)(2,1)}, u32[]{:S(2)}) copy-start(bf16[2,640,128]{2,1,0:T(8,128)(2,1)} %get-tuple-element.16) | copy-start | bytes 983044
  60.4 2.1 %collective-permute-start.13 = (bf16[512,512]{1,0:T(8,128)(2,1)}, bf16[512,512]{1,0:T(8,128)(2,1)S(1)}, u32[]{:S(2)}, u32[]{:S(2)}) collective-permute-start(bf16[512,512]{1,0:T(8,128)(2,1)} %collective-permute-done.10), channel_id=1, source_target_pairs={{0,1},{1,0},{2,3},{3,2},{4,5},{5,4},{6,7},{7,6},{8,9},{9,8},{10,11... | collective-permute-start | bytes 1572872 | tf_op jit(solution)/shard_map/ppermute | solution.py:194
  60.4 10.4 %collective-permute-start.9 = (bf16[2,640,128]{2,1,0:T(8,128)(2,1)}, bf16[2,640,128]{2,1,0:T(8,128)(2,1)}, u32[]{:S(2)}, u32[]{:S(2)}) collective-permute-start(bf16[2,640,128]{2,1,0:T(8,128)(2,1)} %get-tuple-element.17), channel_id=1, source_target_pairs={{0,16},{8,24},{16,0},{24,8},{1,17},{9,25},{17,1},{25,9},{2,18},{10... | collective-permute-start | bytes 983048 | tf_op jit(solution)/shard_map/ppermute | solution.py:188
  60.9 9.9 %collective-permute-start.8 = (bf16[2,640,128]{2,1,0:T(8,128)(2,1)S(1)}, bf16[2,640,128]{2,1,0:T(8,128)(2,1)}, u32[]{:S(2)}, u32[]{:S(2)}) collective-permute-start(bf16[2,640,128]{2,1,0:T(8,128)(2,1)S(1)} %copy-done.8), channel_id=1, source_target_pairs={{0,8},{8,0},{16,24},{24,16},{1,9},{9,1},{17,25},{25,17},{2,10},{10... | collective-permute-start | bytes 983048 | tf_op jit(solution)/shard_map/ppermute | solution.py:185
  62.5 1.6 %copy-start.1 = (bf16[17,512,128]{2,1,0:T(8,128)(2,1)S(1)}, bf16[17,512,128]{2,1,0:T(8,128)(2,1)}, u32[]{:S(2)}) copy-start(bf16[17,512,128]{2,1,0:T(8,128)(2,1)} %halves.1.refs_3_) | copy-start | bytes 6684676
